TPU v7x, 32 devices: a whole 2x2x4 slice. The times are simulated.
32 devices in a mesh: ctx: 8 (over z, y), tp: 4 (over x, core).
Axes of the slice: x: 2, y: 2, z: 4, core: 2. Of those that a mesh axis runs over, the one named last changes fastest.
Arguments:
- query_proj: bfloat16 [1024, 4096], P('ctx', 'tp'), may hold values from -6 to 6
- key_proj: bfloat16 [1024, 4096], P('ctx', 'tp'), may hold values from -6 to 6
- value_proj: bfloat16 [1024, 4096], P('ctx', 'tp'), may hold values from -6 to 6
- filters: float32 [256, 128], P('tp'), may hold values from -0.5 to 0.5
- skip_gain: float32 [4096], P('tp'), may hold values from -1 to 1
- out_grad: bfloat16 [1024, 4096], P('ctx', 'tp'), may hold values from -6 to 6
- w_out: bfloat16 [4096, 4096], P('tp'), may hold values from -0.09375 to 0.09375
Outputs:
- query_grad: bfloat16 [1024, 4096], P('ctx', 'tp')
- key_grad: bfloat16 [1024, 4096], P('ctx', 'tp')
- value_grad: bfloat16 [1024, 4096], P('ctx', 'tp')
- filter_grad: float32 [256, 128], P('tp')
- skip_grad: float32 [4096], P('tp')
All inputs are finite; a program needn't handle non-finite values.
Results may differ from a plain program's by a relative error of at most 0.0075.
Values may be sent and summed in bfloat16 or wider, within the bound.
A program may use at most 128 MiB of HBM per device.

v0:
```python
import jax
import jax.numpy as jnp
from jax import lax
from jax.sharding import PartitionSpec as P


def passed_along(block, axis, distance):
    devices = range(lax.axis_size(axis))
    route = [(i - distance, i) for i in devices if i - distance in devices]
    return lax.ppermute(block, axis, route)


def blocks_of(extended, width):
    count = (extended.shape[0] - width) // width
    channels = extended.shape[1]
    first = extended[:-width].reshape(count, width, channels)
    second = extended[width:].reshape(count, width, channels)
    return jnp.concatenate([first, second], axis=1)


def tap_table(filters, causal):
    width = filters.shape[1]
    rows = jnp.arange(width)[:, None]
    cols = jnp.arange(2 * width)[None, :]
    lag = rows + width - cols if causal else cols - rows
    valid = (lag >= 0) & (lag < width)
    index = jnp.clip(lag, 0, width - 1)
    table = filters[:, index]
    return jnp.where(valid[None], table, jnp.float32(0.0))


def convolve(extended, filters, skip_gain, causal):
    width = filters.shape[1]
    groups = filters.shape[0]
    channels = extended.shape[1]
    window = blocks_of(extended, width)
    count = window.shape[0]
    window = window.reshape(count, 2 * width, groups, channels // groups).astype(jnp.float32)
    mixed = jnp.einsum(
        "gij,bjgc->bigc", tap_table(filters, causal), window, precision=lax.Precision.HIGHEST
    )
    mixed = mixed.reshape(count * width, channels)
    current = extended[width:] if causal else extended[:-width]
    return mixed + skip_gain[None, :] * current.astype(jnp.float32)


def diagonal_lags(pairs, width):
    leading = pairs.shape[:-2]
    flat = pairs.reshape(leading + (width * 2 * width,))
    padded = jnp.concatenate([flat, jnp.zeros(leading + (width,), jnp.float32)], axis=-1)
    skewed = padded.reshape(leading + (width, 2 * width + 1)).sum(axis=-2)
    return skewed[..., width:0:-1]


def on_device(query_proj, key_proj, value_proj, filters, skip_gain, out_grad, w_out):
    width = filters.shape[1]
    groups = filters.shape[0]
    tok_rows = query_proj.shape[0]
    channels = query_proj.shape[1]
    span = channels // groups
    rim_rows = width - 1
    count = tok_rows // width
    query_f = query_proj.astype(jnp.float32)
    key_f = key_proj.astype(jnp.float32)
    value_f = value_proj.astype(jnp.float32)
    products = (key_f * value_f).astype(jnp.bfloat16)
    product_f = products.astype(jnp.float32)
    mixer_grad = lax.dot_general(
        lax.all_gather(out_grad, "tp", axis=1, tiled=True),
        w_out,
        (((1,), (1,)), ((), ())),
        preferred_element_type=jnp.float32,
    )
    earlier = passed_along(products[tok_rows - rim_rows :], "ctx", 1)
    single = jnp.zeros((1, channels), jnp.bfloat16)
    prod_ext = jnp.concatenate([single, earlier, products], axis=0)
    filtered = convolve(prod_ext, filters, skip_gain, True)
    query_grad = (mixer_grad * filtered).astype(jnp.bfloat16)
    filtered_grad = (mixer_grad * query_f).astype(jnp.bfloat16)
    grad_f = filtered_grad.astype(jnp.float32)
    later = passed_along(filtered_grad[:rim_rows], "ctx", -1)
    grad_ext = jnp.concatenate([filtered_grad, later, single], axis=0)
    product_grad = convolve(grad_ext, filters, skip_gain, False)
    key_grad = (product_grad * value_f).astype(jnp.bfloat16)
    value_grad = (product_grad * key_f).astype(jnp.bfloat16)
    window = blocks_of(prod_ext, width)
    grad_blocks = filtered_grad.reshape(count, width, channels)
    skip_part = jnp.sum(grad_f * product_f, axis=0)
    pairs = jnp.einsum(
        "bigc,bjgc->gij",
        grad_blocks.reshape(count, width, groups, span),
        window.reshape(count, 2 * width, groups, span),
        preferred_element_type=jnp.float32,
    )
    grouped = diagonal_lags(pairs, width)
    filter_grad, skip_grad = lax.psum((grouped, skip_part), "ctx")
    return (query_grad, key_grad, value_grad, filter_grad, skip_grad)


def solution(mesh):
    return jax.shard_map(
        on_device,
        mesh=mesh,
        in_specs=(
            P("ctx", "tp"),
            P("ctx", "tp"),
            P("ctx", "tp"),
            P("tp", None),
            P("tp"),
            P("ctx", "tp"),
            P("tp", None),
        ),
        out_specs=(P("ctx", "tp"), P("ctx", "tp"), P("ctx", "tp"), P("tp", None), P("tp")),
        check_vma=False,
    )
```

profile of v0, /device:TPU:0, one launch (start us, length us, event | category | flops | bytes accessed | tf_op | source)
XLA Modules:
  0.0 376.2 jit_solution(13880040861033989793)
XLA Ops:
  7.2 0.0 copy-start.2
  7.2 0.0 all-gather.2.cloned.1.call-start
  7.2 0.7 all-gather.2.cloned.1.call-update
  8.0 0.1 copy.37
  8.0 0.1 fusion.21
  8.1 0.1 copy.36
  8.3 20.7 %all-gather.2.cloned.1.call-done = bf16[128,4096]{1,0:T(8,128)(2,1)} async-done(((bf16[128,1024]{1,0:T(8,128)(2,1)}), bf16[128,4096]{1,0:T(8,128)(2,1)}) %all-gather.2.cloned.1.call-update) | async-done | bytes 1048592 | tf_op jit(solution)/shard_map/all_gather | solution.py:69
  29.0 6.7 %fusion.17 = (f32[1024]{0:T(1024)S(1)}, bf16[128,1024]{1,0:T(8,128)(2,1)S(1)}, bf16[128,1024]{1,0:T(8,128)(2,1)S(1)}, f32[128,1024]{1,0:T(8,128)S(1)}) fusion(bf16[128,1024]{1,0:T(8,128)(2,1)} %param.7, bf16[128,1024]{1,0:T(8,128)(2,1)} %param.9, bf16[128,1024]{1,0:T(8,128)(2,1)} %param.8, bf16[128,4096]{1,0:T(8,128)(2,1)} %all-gather.2.cloned.1.call-done, ...), kind=kOutput, calls=%fused_computation.25 | convolution fusion | flops 1075182592 | bytes 11276288 | tf_op jit(solution)/shard_map/dot_general | solution.py:68
  35.8 1.3 collective-permute-start.1
  37.1 0.0 copy-done.2
  37.1 0.1 copy.25
  37.2 108.4 %gather_fusion.1 = f32[32768,64]{1,0:T(8,128)} fusion(f32[64,128]{0,1:T(8,128)S(1)} %copy.25, s32[32768]{0:T(1024)S(1)} %broadcast_clamp_fusion), kind=kCustom, calls=%fused_computation.1 | custom fusion | bytes 16908288 | tf_op jit(solution)/shard_map/gather | solution.py:28
  145.6 13.6 %copy.31 = f32[128,256,64]{1,0,2:T(8,128)} copy(f32[128,256,64]{2,1,0:T(8,128)} %bitcast.45) | data formatting | bytes 16777216 | tf_op jit(solution)/shard_map/gather | solution.py:28
  159.2 108.3 %gather_fusion = f32[32768,64]{1,0:T(8,128)} fusion(f32[64,128]{0,1:T(8,128)S(1)} %copy.25, s32[32768]{0:T(1024)S(1)} %broadcast_clamp_fusion.1), kind=kCustom, calls=%fused_computation | custom fusion | bytes 16908288 | tf_op jit(solution)/shard_map/gather | solution.py:28
  267.5 13.6 %copy.26 = f32[128,256,64]{1,0,2:T(8,128)} copy(f32[128,256,64]{2,1,0:T(8,128)} %bitcast.44) | data formatting | bytes 16777216 | tf_op jit(solution)/shard_map/gather | solution.py:28
  281.1 0.1 fusion.27
  281.2 0.2 copy.28
  281.4 0.2 copy.24
  281.6 0.1 slice.19
  281.6 4.7 %collective-permute-start = (bf16[127,1024]{1,0:T(8,128)(2,1)S(1)}, bf16[127,1024]{1,0:T(8,128)(2,1)S(1)}, u32[]{:S(2)}, u32[]{:S(2)}) collective-permute-start(bf16[127,1024]{1,0:T(8,128)(2,1)S(1)} %slice.19), channel_id=1, source_target_pairs={{0,4},{4,8},{8,12},{12,16},{16,20},{20,24},{24,28},{1,5},{5,9},{9,... | collective-permute-start | bytes 780296 | tf_op jit(solution)/shard_map/ppermute | solution.py:10
  286.4 0.0 collective-permute-done.1
  286.4 0.2 copy.35
  286.6 0.1 concatenate.32.clone
  286.6 6.5 %fusion = f32[64,16,128]{2,1,0:T(8,128)S(1)} fusion(f32[128,256,64]{1,0,2:T(8,128)} %copy.31, pred[128,256]{1,0:T(8,128)(4,1)S(1)} %fusion.28, bf16[1,128,64,16]{1,3,2,0:T(8,128)(2,1)S(1)} %bitcast.57, bf16[1,128,64,16]{1,3,2,0:T(8,128)(2,1)S(1)} %bitcast.50), kind=kOutput, calls=%fused_computation.2 | convolution fusion | flops 405798912 | bytes 9469952 | tf_op jit(solution)/shard_map/gij,bjgc->bigc/dot_general | solution.py:39
  293.2 0.2 copy.32
  293.4 0.0 collective-permute-done
  293.4 0.2 copy.34
  293.6 0.1 concatenate.27.clone
  293.7 6.5 %fusion.2 = f32[64,16,128]{2,1,0:T(8,128)S(1)} fusion(f32[128,256,64]{1,0,2:T(8,128)} %copy.26, pred[128,256]{1,0:T(8,128)(4,1)S(1)} %fusion.27, bf16[1,128,64,16]{1,3,2,0:T(8,128)(2,1)S(1)} %bitcast.52, bf16[1,128,64,16]{1,3,2,0:T(8,128)(2,1)S(1)} %bitcast.48), kind=kOutput, calls=%fused_computation.4 | convolution fusion | flops 405798912 | bytes 9469952 | tf_op jit(solution)/shard_map/gij,bjgc->bigc/dot_general | solution.py:39
  300.3 0.2 copy.27
  300.5 1.3 fusion.20
  301.8 4.7 %copy.38 = f32[8,8,128,256]{3,1,2,0:T(8,128)S(1)} copy(f32[8,8,128,256]{3,2,1,0:T(8,128)S(1)} %bitcast.47) | data formatting | bytes 16777216
  306.5 3.8 concatenate.35
  310.3 14.2 %reshape.171 = f32[64,128,257]{2,1,0:T(8,128)} reshape(f32[64,32896]{1,0:T(8,128)} %concatenate.35) | data formatting | bytes 16842752 | tf_op jit(solution)/shard_map/reshape | solution.py:51
  324.4 0.0 copy-start
  324.4 0.0 copy-start.1
  324.4 0.0 copy-start.3
  324.4 6.1 %reduce_sum.18 = f32[64,257]{1,0:T(8,128)S(1)} reduce(f32[64,128,257]{2,1,0:T(8,128)} %reshape.171, f32[]{:T(128)} %constant.1.clone.1), dimensions={1}, to_apply=%region_0.1 | reduce | flops 2088896 | bytes 8487172 | tf_op jit(solution)/shard_map/reduce_sum | solution.py:51
  330.6 0.1 slice.21
  330.7 0.1 rev.3
  330.7 37.5 %all-reduce.3 = (f32[64,128]{1,0:T(8,128)}, f32[1024]{0:T(1024)}) all-reduce(f32[64,128]{1,0:T(8,128)S(1)} %rev.3, f32[1024]{0:T(1024)S(1)} %get-tuple-element.7), channel_id=1, replica_groups=mesh['ctx'=8,'tp'=4] {'ctx'}, use_global_device_ids=true, to_apply=%region_1.2 | all-reduce | flops 9216 | bytes 73728 | tf_op jit(solution)/shard_map/psum | solution.py:96
  368.2 0.0 copy-done
  368.2 0.0 copy-done.1
  368.3 0.0 copy-done.3
  368.3 1.1 fusion.10
  (5 shorter events, 0.1 us)
Async XLA Ops:
  7.2 29.9 %copy-start.2 = (f32[64,128]{1,0:T(8,128)S(1)}, f32[64,128]{1,0:T(8,128)}, u32[]{:S(2)}) copy-start(f32[64,128]{1,0:T(8,128)} %param.10) | copy-start | bytes 98308
  7.2 21.9 %all-gather.2.cloned.1.call-start = ((), (), s32[]{:S(2)}) async-start(), calls=%async_computation | async-start | bytes 1310720 | tf_op jit(solution)/shard_map/all_gather | solution.py:69
  35.8 250.6 %collective-permute-start.1 = (bf16[127,1024]{1,0:T(8,128)(2,1)S(1)}, bf16[127,1024]{1,0:T(8,128)(2,1)S(1)}, u32[]{:S(2)}, u32[]{:S(2)}) collective-permute-start(bf16[127,1024]{1,0:T(8,128)(2,1)S(1)} %bitcast.54), channel_id=1, source_target_pairs={{4,0},{8,4},{12,8},{16,12},{20,16},{24,20},{28,24},{5,1},{9,5},{13... | collective-permute-start | bytes 780296 | tf_op jit(solution)/shard_map/ppermute | solution.py:10
  281.6 11.8 %collective-permute-start = (bf16[127,1024]{1,0:T(8,128)(2,1)S(1)}, bf16[127,1024]{1,0:T(8,128)(2,1)S(1)}, u32[]{:S(2)}, u32[]{:S(2)}) collective-permute-start(bf16[127,1024]{1,0:T(8,128)(2,1)S(1)} %slice.19), channel_id=1, source_target_pairs={{0,4},{4,8},{8,12},{12,16},{16,20},{20,24},{24,28},{1,5},{5,9},{9,... | collective-permute-start | bytes 780296 | tf_op jit(solution)/shard_map/ppermute | solution.py:10
  324.4 43.8 %copy-start = (bf16[128,1024]{1,0:T(8,128)(2,1)S(1)}, bf16[128,1024]{1,0:T(8,128)(2,1)}, u32[]{:S(2)}) copy-start(bf16[128,1024]{1,0:T(8,128)(2,1)} %param.8) | copy-start | bytes 786436
  324.4 43.8 %copy-start.1 = (bf16[128,1024]{1,0:T(8,128)(2,1)S(1)}, bf16[128,1024]{1,0:T(8,128)(2,1)}, u32[]{:S(2)}) copy-start(bf16[128,1024]{1,0:T(8,128)(2,1)} %param.9) | copy-start | bytes 786436
  324.4 43.8 %copy-start.3 = (f32[1024]{0:T(1024)S(1)}, f32[1024]{0:T(1024)}, u32[]{:S(2)}) copy-start(f32[1024]{0:T(1024)} %param.11) | copy-start | bytes 12292
Sparse Core Ops, SparseCore 0:
  9.6 19.4 all-gather.1
where the time goes:
time: 377 us; the launch traced here: 376 us
  local copies, waits for them, and re-layouts  268 us (71%)
  blocking collectives  37.5 us (10%)
  waiting for transfers between devices  21.4 us (6%)
  matrix products  21.1 us (6%)
  between operations  14.2 us (4%)
  other arithmetic  7.52 us (2%)
  starting transfers between devices  6.07 us (2%)
    gather x4, local copies, waits for them, and re-layouts, tap_table(): table = filters[:, index]  244 us
    psum x1, blocking collectives, on_device(): filter_grad, skip_grad = lax.psum((grouped, skip_part), 'ctx')  37.5 us
    all_gather x1, waiting for transfers between devices, on_device(): lax.all_gather(out_grad, 'tp', axis=1, tiled=True)  20.7 us
    reshape x1, local copies, waits for them, and re-layouts, diagonal_lags(): skewed = padded.reshape(leading + (width, 2 * width + 1)).sum(axis=-2)  14.2 us
    dot_general x2, matrix products, convolve(): jnp.einsum('gij,bjgc->bigc', tap_table(filters, causal), window, precisio...  13.1 us
  transfers between devices with their start and end apart: 3, of which 1 were waited for; matrix products, arithmetic and copies ran while one was open for 67% of the time, Pallas kernels for 0%

commit v1 on v0

--- a/solution.py
+++ b/solution.py
@@ -2,6 +2,29 @@
 import jax.numpy as jnp
 from jax import lax
 from jax.sharding import PartitionSpec as P
+
+
+def desk_bring(x_in, axis_id):
+    local_part = jax.lax.axis_size(axis_id)
+    b_next, y_new, high = (local_part, jax.lax.axis_index(axis_id), x_in.shape[1])
+    built = map(lambda dev_j: (dev_j, (dev_j + 1) % b_next), range(b_next))
+    log = list(built)
+    views = list(map(lambda dev_j: (dev_j, (dev_j - 1) % b_next), range(b_next)))
+    big = jnp.zeros((*x_in.shape[:1], b_next * high, *x_in.shape[2:]), x_in.dtype)
+    big = lax.dynamic_update_slice_in_dim(big, x_in, y_new * high, axis=1)
+    long_array = heard = x_in
+    all_rows = b_next // 2
+    for tick in range(1, all_rows + 1):
+        long_array = jax.lax.ppermute(long_array, axis_id, log)
+        big = lax.dynamic_update_slice_in_dim(
+            big, long_array, (y_new - tick) % b_next * high, axis=1
+        )
+        if tick < b_next - all_rows:
+            heard = jax.lax.ppermute(heard, axis_id, views)
+            big = lax.dynamic_update_slice_in_dim(
+                big, heard, (y_new + tick) % b_next * high, axis=1
+            )
+    return big
 
 
 def passed_along(block, axis, distance):
@@ -66,7 +89,7 @@
     products = (key_f * value_f).astype(jnp.bfloat16)
     product_f = products.astype(jnp.float32)
     mixer_grad = lax.dot_general(
-        lax.all_gather(out_grad, "tp", axis=1, tiled=True),
+        desk_bring(out_grad, axis_id="tp"),
         w_out,
         (((1,), (1,)), ((), ())),
         preferred_element_type=jnp.float32,

time: 377 us -> 359 us (0.952)
  waiting for transfers between devices: 21.4 us -> 5.95 us
  between operations: 14.2 us -> 0.95 us
  starting transfers between devices: 6.07 us -> 12.3 us
  local copies, waits for them, and re-layouts: 268 us -> 272 us
    all_gather x1 -> x0, waiting for transfers between devices: 20.7 us -> none  [on_device(): lax.all_gather(out_grad, 'tp', axis=1, tiled=True)]
    ppermute x0 -> x3, waiting for transfers between devices: none -> 5.95 us  [the longest x2 5.95 us: desk_bring(): long_array = jax.lax.ppermute(long_array, axis_id, log)]
    ppermute x0 -> x3, starting transfers between devices: none -> 5.11 us  [the longest x2 3.12 us: desk_bring(): long_array = jax.lax.ppermute(long_array, axis_id, log)]
  transfers between devices with their start and end apart: 3 -> 5, of which waited for: 1 -> 2; matrix products, arithmetic and copies ran while one was open for 67% -> 71% of each run, Pallas kernels for 0% -> 0%
where the time goes in v1:
time: 359 us; the launch traced here: 358 us
  local copies, waits for them, and re-layouts  272 us (76%)
  blocking collectives  38.4 us (11%)
  matrix products  20.7 us (6%)
  starting transfers between devices  12.3 us (3%)
  other arithmetic  7.55 us (2%)
  waiting for transfers between devices  5.95 us (2%)
    gather x4, local copies, waits for them, and re-layouts, tap_table(): table = filters[:, index]  245 us
    psum x1, blocking collectives, on_device(): filter_grad, skip_grad = lax.psum((grouped, skip_part), 'ctx')  38.4 us
    reshape x1, local copies, waits for them, and re-layouts, diagonal_lags(): skewed = padded.reshape(leading + (width, 2 * width + 1)).sum(axis=-2)  14.2 us
    dot_general x2, matrix products, convolve(): jnp.einsum('gij,bjgc->bigc', tap_table(filters, causal), window, precisio...  13.1 us
  transfers between devices with their start and end apart: 5, of which 2 were waited for; matrix products, arithmetic and copies ran while one was open for 71% of the time, Pallas kernels for 0%

profile of v1, /device:TPU:0, one launch (start us, length us, event | category | flops | bytes accessed | tf_op | source)
XLA Modules:
  0.0 358.1 jit_solution(17149208482503832707)
XLA Ops:
  0.6 0.0 copy-start.3
  0.6 0.5 collective-permute-start
  1.1 2.0 collective-permute-start.1
  3.2 0.1 copy.37
  3.3 0.1 fusion.21
  3.4 0.1 copy.36
  3.5 4.0 %collective-permute-done = bf16[128,1024]{1,0:T(8,128)(2,1)S(1)} collective-permute-done((bf16[128,1024]{1,0:T(8,128)(2,1)}, bf16[128,1024]{1,0:T(8,128)(2,1)S(1)}, u32[]{:S(2)}, u32[]{:S(2)}) %collective-permute-start) | collective-permute-done | bytes 262176 | tf_op jit(solution)/shard_map/ppermute | solution.py:18
  7.5 2.6 collective-permute-start.2
  10.1 0.1 broadcast_in_dim.20
  10.2 1.0 constant_dynamic-update-slice_fusion.3
  11.3 0.0 collective-permute-done.1
  11.3 2.0 collective-permute-done.2
  13.3 6.4 %fusion.17 = (f32[1024]{0:T(1024)S(1)}, bf16[128,1024]{1,0:T(8,128)(2,1)S(1)}, bf16[128,1024]{1,0:T(8,128)(2,1)S(1)}, f32[128,1024]{1,0:T(8,128)S(1)}) fusion(bf16[128,1024]{1,0:T(8,128)(2,1)} %param.7, bf16[128,1024]{1,0:T(8,128)(2,1)} %param.9, bf16[128,1024]{1,0:T(8,128)(2,1)} %param.8, bf16[128,4096]{1,0:T(8,128)(2,1)S(1)} %constant_dynamic-update-slice_fusion, ...), kind=kOutput, calls=%fused_computation.25 | convolution fusion | flops 1075182592 | bytes 11276288 | tf_op jit(solution)/shard_map/dot_general | solution.py:91
  19.7 1.3 collective-permute-start.4
  21.1 0.0 copy-done.3
  21.1 0.1 copy.25
  21.2 109.0 %gather_fusion.1 = f32[32768,64]{1,0:T(8,128)} fusion(f32[64,128]{0,1:T(8,128)S(1)} %copy.25, s32[32768]{0:T(1024)S(1)} %broadcast_clamp_fusion), kind=kCustom, calls=%fused_computation.1 | custom fusion | bytes 16908288 | tf_op jit(solution)/shard_map/gather | solution.py:51
  130.1 13.6 %copy.31 = f32[128,256,64]{1,0,2:T(8,128)} copy(f32[128,256,64]{2,1,0:T(8,128)} %bitcast.45) | data formatting | bytes 16777216 | tf_op jit(solution)/shard_map/gather | solution.py:51
  143.8 109.0 %gather_fusion = f32[32768,64]{1,0:T(8,128)} fusion(f32[64,128]{0,1:T(8,128)S(1)} %copy.25, s32[32768]{0:T(1024)S(1)} %broadcast_clamp_fusion.1), kind=kCustom, calls=%fused_computation | custom fusion | bytes 16908288 | tf_op jit(solution)/shard_map/gather | solution.py:51
  252.7 13.6 %copy.26 = f32[128,256,64]{1,0,2:T(8,128)} copy(f32[128,256,64]{2,1,0:T(8,128)} %bitcast.44) | data formatting | bytes 16777216 | tf_op jit(solution)/shard_map/gather | solution.py:51
  266.3 0.1 fusion.27
  266.5 0.2 copy.28
  266.6 0.2 copy.24
  266.8 0.8 slice.19
  267.6 5.9 %collective-permute-start.3 = (bf16[127,1024]{1,0:T(8,128)(2,1)}, bf16[127,1024]{1,0:T(8,128)(2,1)S(1)}, u32[]{:S(2)}, u32[]{:S(2)}) collective-permute-start(bf16[127,1024]{1,0:T(8,128)(2,1)} %slice.19), channel_id=1, source_target_pairs={{0,4},{4,8},{8,12},{12,16},{16,20},{20,24},{24,28},{1,5},{5,9},{9,... | collective-permute-start | bytes 780296 | tf_op jit(solution)/shard_map/ppermute | solution.py:33
  273.4 0.0 collective-permute-done.4
  273.5 0.2 copy.35
  273.6 0.1 concatenate.32.clone
  273.7 6.5 %fusion = f32[64,16,128]{2,1,0:T(8,128)S(1)} fusion(f32[128,256,64]{1,0,2:T(8,128)} %copy.31, pred[128,256]{1,0:T(8,128)(4,1)S(1)} %fusion.28, bf16[1,128,64,16]{1,3,2,0:T(8,128)(2,1)S(1)} %bitcast.57, bf16[1,128,64,16]{1,3,2,0:T(8,128)(2,1)S(1)} %bitcast.50), kind=kOutput, calls=%fused_computation.2 | convolution fusion | flops 405798912 | bytes 9469952 | tf_op jit(solution)/shard_map/gij,bjgc->bigc/dot_general | solution.py:62
  280.2 0.2 copy.32
  280.4 0.0 collective-permute-done.3
  280.5 0.2 copy.34
  280.6 0.1 concatenate.27.clone
  280.8 6.5 %fusion.2 = f32[64,16,128]{2,1,0:T(8,128)S(1)} fusion(f32[128,256,64]{1,0,2:T(8,128)} %copy.26, pred[128,256]{1,0:T(8,128)(4,1)S(1)} %fusion.27, bf16[1,128,64,16]{1,3,2,0:T(8,128)(2,1)S(1)} %bitcast.52, bf16[1,128,64,16]{1,3,2,0:T(8,128)(2,1)S(1)} %bitcast.48), kind=kOutput, calls=%fused_computation.4 | convolution fusion | flops 405798912 | bytes 9469952 | tf_op jit(solution)/shard_map/gij,bjgc->bigc/dot_general | solution.py:62
  287.3 1.0 copy.27
  288.3 1.3 fusion.20
  289.6 4.7 %copy.38 = f32[8,8,128,256]{3,1,2,0:T(8,128)S(1)} copy(f32[8,8,128,256]{3,2,1,0:T(8,128)S(1)} %bitcast.47) | data formatting | bytes 16777216
  294.4 3.7 %concatenate.35 = f32[64,32896]{1,0:T(8,128)} pad(f32[64,32768]{1,0:T(8,128)S(1)} %bitcast.46, f32[]{:T(128)} %constant.48.clone.1), padding=0_0x0_128 | pad | bytes 16809988 | tf_op jit(solution)/shard_map/concatenate | solution.py:73
  298.1 14.2 %reshape.171 = f32[64,128,257]{2,1,0:T(8,128)} reshape(f32[64,32896]{1,0:T(8,128)} %concatenate.35) | data formatting | bytes 16842752 | tf_op jit(solution)/shard_map/reshape | solution.py:74
  312.3 6.2 %reduce_sum.18 = f32[64,257]{1,0:T(8,128)S(1)} reduce(f32[64,128,257]{2,1,0:T(8,128)} %reshape.171, f32[]{:T(128)} %constant.48.clone.1), dimensions={1}, to_apply=%region_0.1 | reduce | flops 2088896 | bytes 8487172 | tf_op jit(solution)/shard_map/reduce_sum | solution.py:74
  318.5 0.1 slice.21
  318.5 0.1 rev.3
  318.6 38.4 %all-reduce.3 = (f32[64,128]{1,0:T(8,128)}, f32[1024]{0:T(1024)}) all-reduce(f32[64,128]{1,0:T(8,128)S(1)} %rev.3, f32[1024]{0:T(1024)S(1)} %get-tuple-element.7), channel_id=1, replica_groups=mesh['ctx'=8,'tp'=4] {'ctx'}, use_global_device_ids=true, to_apply=%region_1.2 | all-reduce | flops 9216 | bytes 73728 | tf_op jit(solution)/shard_map/psum | solution.py:119
  357.0 0.0 copy-done
  357.0 0.0 copy-done.1
  357.0 0.0 copy-done.2
  357.0 0.0 copy-done.4
  357.0 1.1 fusion.10
  (12 shorter events, 0.2 us)
Async XLA Ops:
  0.6 20.4 %copy-start.3 = (f32[64,128]{1,0:T(8,128)S(1)}, f32[64,128]{1,0:T(8,128)}, u32[]{:S(2)}) copy-start(f32[64,128]{1,0:T(8,128)} %param.10) | copy-start | bytes 98308
  0.6 6.8 %collective-permute-start = (bf16[128,1024]{1,0:T(8,128)(2,1)}, bf16[128,1024]{1,0:T(8,128)(2,1)S(1)}, u32[]{:S(2)}, u32[]{:S(2)}) collective-permute-start(bf16[128,1024]{1,0:T(8,128)(2,1)} %param.12), channel_id=1, source_target_pairs={{0,1},{1,2},{2,3},{3,0},{4,5},{5,6},{6,7},{7,4},{8,9},{9,10},{10,1... | collective-permute-start | bytes 786440 | tf_op jit(solution)/shard_map/ppermute | solution.py:18
  1.1 10.1 %collective-permute-start.1 = (bf16[128,1024]{1,0:T(8,128)(2,1)}, bf16[128,1024]{1,0:T(8,128)(2,1)S(1)}, u32[]{:S(2)}, u32[]{:S(2)}) collective-permute-start(bf16[128,1024]{1,0:T(8,128)(2,1)} %param.12), channel_id=1, source_target_pairs={{0,3},{1,0},{2,1},{3,2},{4,7},{5,4},{6,5},{7,6},{8,11},{9,8},{10,9... | collective-permute-start | bytes 786440 | tf_op jit(solution)/shard_map/ppermute | solution.py:23
  7.5 5.8 %collective-permute-start.2 = (bf16[128,1024]{1,0:T(8,128)(2,1)S(1)}, bf16[128,1024]{1,0:T(8,128)(2,1)S(1)}, u32[]{:S(2)}, u32[]{:S(2)}) collective-permute-start(bf16[128,1024]{1,0:T(8,128)(2,1)S(1)} %collective-permute-done), channel_id=1, source_target_pairs={{0,1},{1,2},{2,3},{3,0},{4,5},{5,6},{6,7},{7,4},{8,9},{9,10},{10,1... | collective-permute-start | bytes 786440 | tf_op jit(solution)/shard_map/ppermute | solution.py:18
  19.7 253.7 %collective-permute-start.4 = (bf16[127,1024]{1,0:T(8,128)(2,1)S(1)}, bf16[127,1024]{1,0:T(8,128)(2,1)S(1)}, u32[]{:S(2)}, u32[]{:S(2)}) collective-permute-start(bf16[127,1024]{1,0:T(8,128)(2,1)S(1)} %bitcast.54), channel_id=1, source_target_pairs={{4,0},{8,4},{12,8},{16,12},{20,16},{24,20},{28,24},{5,1},{9,5},{13... | collective-permute-start | bytes 780296 | tf_op jit(solution)/shard_map/ppermute | solution.py:33
  267.6 12.9 %collective-permute-start.3 = (bf16[127,1024]{1,0:T(8,128)(2,1)}, bf16[127,1024]{1,0:T(8,128)(2,1)S(1)}, u32[]{:S(2)}, u32[]{:S(2)}) collective-permute-start(bf16[127,1024]{1,0:T(8,128)(2,1)} %slice.19), channel_id=1, source_target_pairs={{0,4},{4,8},{8,12},{12,16},{16,20},{20,24},{24,28},{1,5},{5,9},{9,... | collective-permute-start | bytes 780296 | tf_op jit(solution)/shard_map/ppermute | solution.py:33
  312.3 44.7 %copy-start = (f32[128,1024]{1,0:T(8,128)S(1)}, f32[128,1024]{1,0:T(8,128)}, u32[]{:S(2)}) copy-start(f32[128,1024]{1,0:T(8,128)} %copy.27) | copy-start | bytes 1572868
  312.3 44.7 %copy-start.1 = (bf16[128,1024]{1,0:T(8,128)(2,1)S(1)}, bf16[128,1024]{1,0:T(8,128)(2,1)}, u32[]{:S(2)}) copy-start(bf16[128,1024]{1,0:T(8,128)(2,1)} %param.8) | copy-start | bytes 786436
  312.3 44.7 %copy-start.2 = (bf16[128,1024]{1,0:T(8,128)(2,1)S(1)}, bf16[128,1024]{1,0:T(8,128)(2,1)}, u32[]{:S(2)}) copy-start(bf16[128,1024]{1,0:T(8,128)(2,1)} %param.9) | copy-start | bytes 786436
  312.3 44.7 %copy-start.4 = (f32[1024]{0:T(1024)S(1)}, f32[1024]{0:T(1024)}, u32[]{:S(2)}) copy-start(f32[1024]{0:T(1024)} %param.11) | copy-start | bytes 12292
